TPU v7x, 512 devices: a whole 4x8x8 slice. The times are simulated.
512 devices in a mesh: ctx: 128 (over x, y, z_hi, core), batch: 4 (over z_lo).
Axes of the slice: x: 4, y: 8, z: 8 (z_hi: 2, z_lo: 4; z = z_hi * 4 + z_lo), core: 2. Of those that a mesh axis runs over, the one named last changes fastest.
Arguments:
- query_rows: bfloat16 [131072, 1024], P(('batch', 'ctx')), parts along dimension 0, may hold values from -6 to 6
- key_rows: bfloat16 [131072, 128], P(('batch', 'ctx')), parts along dimension 0, may hold values from -6 to 6
- value_rows: bfloat16 [131072, 128], P(('batch', 'ctx')), parts along dimension 0, may hold values from -6 to 6
- out_grad: bfloat16 [131072, 1024], P(('batch', 'ctx')), parts along dimension 0, may hold values from -6 to 6
- log_norm: float32 [8, 131072], P(None, ('batch', 'ctx')), parts along dimension 1, may hold values from 3 to 5
- row_dot: float32 [8, 131072], P(None, ('batch', 'ctx')), parts along dimension 1, may hold values from -24 to 24
- span_order: int32 [512], P('batch'), parts along dimension 0, may hold values from 0 to 127, each once
Outputs:
- query_grad: bfloat16 [131072, 1024], P(('batch', 'ctx')), parts along dimension 0
- key_grad: bfloat16 [131072, 128], P(('batch', 'ctx')), parts along dimension 0
- value_grad: bfloat16 [131072, 128], P(('batch', 'ctx')), parts along dimension 0
There are 4 independent parts, one for each index of `batch`. A program takes and returns all parts, laid end to end along the dimension named above; each array names one. Nothing has to cross between parts.
Inputs may be any that keep to these rules, and one draw needn't show every extreme that they name: span_order holds every number from 0 to 128 - 1 once.
All inputs are finite; a program needn't handle non-finite values.
Results may differ from a plain program's by a relative error of at most 0.0049.
Values may be sent and summed in bfloat16 or wider, within the bound.
A program may use at most 64 MiB of HBM per device.

v0:
```python
import functools
import math

import jax
import jax.numpy as jnp
from jax import lax
from jax.experimental import pallas as pl
from jax.experimental.pallas import tpu as pltpu
from jax.sharding import PartitionSpec as P

MESH = pl.DeviceIdType.MESH
BF16, F32 = jnp.bfloat16, jnp.float32
NEAR, FAR = 0, 1
OWN_EE, OWN_LE, OWN_LL, PARTNER = 0, 1, 2, 3


def dot_nt(left, right):
    return lax.dot_general(left, right, (((1,), (1,)), ((), ())), preferred_element_type=F32)


def dot_nn(left, right):
    return jnp.dot(left, right, preferred_element_type=F32)


def kernel(
    n, heads, half, width,
    query_hbm, key_hbm, value_hbm, grad_hbm, norm_hbm, dot_hbm, span_hbm,
    query_out, key_out, value_out,
    query, grad, norm, dot, keys, values, span,
    got, part, back, score_grads, own_key, own_value,
    local_sem, span_sem, send_sem, recv_sem, part_send_sem, back_sem,
):
    me = lax.axis_index("ctx")
    right, left = lax.rem(me + 1, n), lax.rem(me + n - 1, n)
    across = lax.rem(me + n // 2, n)
    inv_root = 1.0 / math.sqrt(width)

    barrier = pltpu.get_barrier_semaphore()
    for device in (right, left, across):
        pl.semaphore_signal(barrier, inc=1, device_id={"ctx": device}, device_id_type=MESH)

    loads = []
    for source, target in ((key_hbm, keys), (value_hbm, values), (query_hbm, query), (grad_hbm, grad)):
        for block in range(2):
            loads.append((source.at[pl.ds(block * half, half)], target.at[block]))
    for source, target in ((norm_hbm, norm), (dot_hbm, dot)):
        for block in range(2):
            loads.append((source.at[:, pl.ds(block * half, half)], target.at[block]))
    loads = [
        pltpu.make_async_copy(source, target, local_sem.at[i])
        for i, (source, target) in enumerate(loads)
    ]
    span_load = pltpu.make_async_copy(span_hbm, span, span_sem)
    for load in loads:
        load.start()
    span_load.start()

    def offer(slot, block, which, device):
        source = (key_hbm, value_hbm)[which].at[pl.ds(block * half, half)]
        return pltpu.make_async_remote_copy(
            src_ref=source,
            dst_ref=got.at[slot, block, which],
            send_sem=send_sem.at[slot, block, which],
            recv_sem=recv_sem.at[slot, block, which],
            device_id={"ctx": device},
            device_id_type=MESH,
        )

    pl.semaphore_wait(barrier, 3)
    offers = {}
    for block in range(2):
        for slot, device in ((NEAR, right), (FAR, across)):
            for which in range(2):
                offers[slot, block, which] = offer(slot, block, which, device)
                offers[slot, block, which].start()

    for load in loads:
        load.wait()
    span_load.wait()
    own_span = span[me]

    causal = lax.broadcasted_iota(jnp.int32, (half, 2 * half), 0) <= (
        lax.broadcasted_iota(jnp.int32, (half, 2 * half), 1) % half
    )

    def block_grads(key_block, value_block, at, slot, diagonal):
        key_term = value_term = None
        for pair in range(heads // 2):
            cols = [pl.ds((2 * pair + i) * width, width) for i in range(2)]
            rows = [pl.ds(2 * pair + i, 1) for i in range(2)]
            query_two = jnp.concatenate([query[at, :, c] for c in cols], axis=0)
            grad_two = jnp.concatenate([grad[at, :, c] for c in cols], axis=0)
            norm_two = jnp.concatenate([norm[at, r, :] for r in rows], axis=1)
            dot_two = jnp.concatenate([dot[at, r, :] for r in rows], axis=1)
            scores = dot_nt(key_block, query_two) * inv_root
            weights = jnp.exp(scores - norm_two)
            if diagonal:
                weights = jnp.where(causal, weights, 0.0)
            prob_grad = dot_nt(value_block, grad_two)
            score_grad = (weights * (prob_grad - dot_two)).astype(BF16)
            score_grads[slot, :, pl.ds(pair * 2 * half, 2 * half)] = score_grad
            value_now = dot_nn(weights.astype(BF16), grad_two)
            key_now = dot_nn(score_grad, query_two)
            value_term = value_now if pair == 0 else value_term + value_now
            key_term = key_now if pair == 0 else key_term + key_now
        return key_term * inv_root, value_term

    key_term, value_term = block_grads(keys[0], values[0], 0, OWN_EE, True)
    key_more, value_more = block_grads(keys[0], values[0], 1, OWN_LE, False)
    own_key[0] = key_term + key_more
    own_value[0] = value_term + value_more
    own_key[1], own_value[1] = block_grads(keys[1], values[1], 1, OWN_LL, True)

    odd = lax.rem(me, 2)

    def partner(step, _):
        slot = lax.rem(step + 1 + odd, 2)
        source = jnp.where(slot == NEAR, left, across)
        other_span = span[source]
        second = jnp.where(other_span < own_span, 0, 1)

        def give(turn, which):
            return pltpu.make_async_remote_copy(
                src_ref=part.at[slot, turn, which],
                dst_ref=back.at[slot, turn, which],
                send_sem=part_send_sem.at[slot, turn, which],
                recv_sem=back_sem.at[slot, turn, which],
                device_id={"ctx": source},
                device_id_type=MESH,
            )

        for turn in range(2):
            for which in range(2):
                pltpu.make_async_copy(
                    got.at[slot, turn, which], got.at[slot, turn, which], recv_sem.at[slot, turn, which]
                ).wait()
            key_block, value_block = got[slot, 0, 0], got[slot, 0, 1]
            if turn == 1:
                key_block = jnp.where(second == 0, key_block, got[slot, 1, 0])
                value_block = jnp.where(second == 0, value_block, got[slot, 1, 1])
            key_term, value_term = block_grads(
                key_block, value_block, second if turn else 1, PARTNER + 2 * slot + turn, False
            )
            part[slot, turn, 0] = key_term.astype(BF16)
            part[slot, turn, 1] = value_term.astype(BF16)
            for which in range(2):
                give(turn, which).start()
        return 0

    lax.fori_loop(0, 2, partner, 0)

    near_early = span[left] < own_span
    far_early = span[across] < own_span

    def second_keys(slot, early):
        return jnp.where(early, got[slot, 0, 0], got[slot, 1, 0])

    zero = jnp.zeros((half, width), BF16)
    near_second, far_second = second_keys(NEAR, near_early), second_keys(FAR, far_early)
    near_slot, far_slot = PARTNER + 2 * NEAR, PARTNER + 2 * FAR
    early_keys = jnp.concatenate(
        [keys[0], jnp.where(near_early, near_second, zero), jnp.where(far_early, far_second, zero)], axis=0
    ).T
    late_keys = jnp.concatenate(
        [
            keys[0], keys[1], got[NEAR, 0, 0], got[FAR, 0, 0],
            jnp.where(near_early, zero, near_second), jnp.where(far_early, zero, far_second),
        ],
        axis=0,
    ).T
    early_slots = (OWN_EE, near_slot + 1, far_slot + 1)
    late_slots = (OWN_LE, OWN_LL, near_slot, far_slot, near_slot + 1, far_slot + 1)
    stores = []
    for pair in range(heads // 2):
        cols = pl.ds(pair * 2 * half, 2 * half)
        for block, (key_side, slots) in enumerate(((early_keys, early_slots), (late_keys, late_slots))):
            scores = jnp.concatenate([score_grads[s, :, cols] for s in slots], axis=0)
            turned = (dot_nn(key_side, scores) * inv_root).astype(BF16)
            for i in range(2):
                query_out[pl.ds(block * half, half), pl.ds((2 * pair + i) * width, width)] = (
                    turned[:, i * half : (i + 1) * half].T
                )

    for slot in (NEAR, FAR):
        for turn in range(2):
            for which in range(2):
                pltpu.make_async_copy(
                    back.at[slot, turn, which], back.at[slot, turn, which], back_sem.at[slot, turn, which]
                ).wait()
    near_first = own_span < span[right]
    far_first = own_span < span[across]
    for which, (own, out) in enumerate(((own_key, key_out), (own_value, value_out))):
        early = own[0] + back[NEAR, 0, which].astype(F32) + back[FAR, 0, which].astype(F32)
        late = own[1]
        for slot, first in ((NEAR, near_first), (FAR, far_first)):
            term = back[slot, 1, which].astype(F32)
            early = early + jnp.where(first, term, 0.0)
            late = late + jnp.where(first, 0.0, term)
        out[pl.ds(0, half)] = early.astype(BF16)
        out[pl.ds(half, half)] = late.astype(BF16)

    for key in offers:
        offers[key].wait_send()
    for slot in (NEAR, FAR):
        for turn in range(2):
            for which in range(2):
                pltpu.make_async_copy(
                    part.at[slot, turn, which], part.at[slot, turn, which], part_send_sem.at[slot, turn, which]
                ).wait()


def place(query_grad, key_grad, value_grad, query_out, key_out, value_out, sem):
    copies = [
        pltpu.make_async_copy(source, target, sem.at[i])
        for i, (source, target) in enumerate(
            ((query_grad, query_out), (key_grad, key_out), (value_grad, value_out))
        )
    ]
    for copy in copies:
        copy.start()
    for copy in copies:
        copy.wait()


def local(query_rows, key_rows, value_rows, out_grad, log_norm, row_dot, span_order):
    n = lax.axis_size("ctx")
    rows, width = key_rows.shape
    heads, half = log_norm.shape[0], rows // 2
    hbm = pl.BlockSpec(memory_space=pltpu.HBM)
    vmem = pl.BlockSpec(memory_space=pltpu.VMEM)
    blocks = 8 * 3 * half * half * heads * 7
    args = (query_rows, key_rows, value_rows, out_grad, log_norm, row_dot, span_order)
    grads = pl.pallas_call(
        functools.partial(kernel, n, heads, half, width),
        name="attention_grads",
        out_shape=(
            pltpu.VMEM(query_rows.shape, BF16),
            pltpu.VMEM(key_rows.shape, BF16),
            pltpu.VMEM(value_rows.shape, BF16),
        ),
        in_specs=[hbm] * 7,
        out_specs=(vmem, vmem, vmem),
        scratch_shapes=[
            pltpu.VMEM((2, half, heads * width), BF16),
            pltpu.VMEM((2, half, heads * width), BF16),
            pltpu.VMEM((2, heads, half), F32),
            pltpu.VMEM((2, heads, half), F32),
            pltpu.VMEM((2, half, width), BF16),
            pltpu.VMEM((2, half, width), BF16),
            pltpu.SMEM((n,), jnp.int32),
            pltpu.VMEM((2, 2, 2, half, width), BF16),
            pltpu.VMEM((2, 2, 2, half, width), BF16),
            pltpu.VMEM((2, 2, 2, half, width), BF16),
            pltpu.VMEM((7, half, heads * half), BF16),
            pltpu.VMEM((2, half, width), F32),
            pltpu.VMEM((2, half, width), F32),
            pltpu.SemaphoreType.DMA((12,)),
            pltpu.SemaphoreType.DMA,
            pltpu.SemaphoreType.DMA((2, 2, 2)),
            pltpu.SemaphoreType.DMA((2, 2, 2)),
            pltpu.SemaphoreType.DMA((2, 2, 2)),
            pltpu.SemaphoreType.DMA((2, 2, 2)),
        ],
        compiler_params=pltpu.CompilerParams(
            collective_id=0, has_side_effects=True, vmem_limit_bytes=24 * 1024 * 1024
        ),
        cost_estimate=pl.CostEstimate(
            flops=10 * half * half * width * heads * 7, bytes_accessed=2 << 20, transcendentals=blocks // 24
        ),
    )(*[pltpu.with_memory_space_constraint(x, pltpu.HBM) for x in args])
    return pl.pallas_call(
        place,
        name="place_grads",
        out_shape=tuple(pltpu.HBM(g.shape, g.dtype) for g in grads),
        in_specs=[vmem] * 3,
        out_specs=(hbm,) * 3,
        scratch_shapes=[pltpu.SemaphoreType.DMA((3,))],
    )(*[pltpu.with_memory_space_constraint(g, pltpu.VMEM) for g in grads])


def solution(mesh):
    return jax.shard_map(
        local,
        mesh=mesh,
        in_specs=(
            P(("batch", "ctx"), None),
            P(("batch", "ctx"), None),
            P(("batch", "ctx"), None),
            P(("batch", "ctx"), None),
            P(None, ("batch", "ctx")),
            P(None, ("batch", "ctx")),
            P("batch"),
        ),
        out_specs=(P(("batch", "ctx"), None), P(("batch", "ctx"), None), P(("batch", "ctx"), None)),
        check_vma=False,
    )
```

profile of v0, /device:TPU:64, one launch (start us, length us, event | category | flops | bytes accessed | tf_op | source)
XLA Modules:
  0.0 26.2 jit_solution(6140482005040422318)
XLA Ops:
  0.6 24.7 %attention_grads.1 = (bf16[256,1024]{1,0:T(8,128)(2,1)S(1)}, bf16[256,128]{1,0:T(8,128)(2,1)S(1)}, bf16[256,128]{1,0:T(8,128)(2,1)S(1)}) custom-call(bf16[256,1024]{1,0:T(8,128)(2,1)} %query_hbm.1, bf16[256,128]{1,0:T(8,128)(2,1)} %key_hbm.1, bf16[256,128]{1,0:T(8,128)(2,1)} %value_hbm.1, bf16[256,1024]{1,0:T(8,128)(2,1)} %grad_hbm.1, f32[8,256]{1,0:T(8,128)} %norm_hbm.1, ...), custom_call_target="tpu_custom_call" | custom-call | flops 1174405120 | bytes 2097152 | tf_op jit(solution)/shard_map/attention_grads/pallas_call | solution.py:233
  25.4 0.9 %place_grads.1 = (bf16[256,1024]{1,0:T(8,128)(2,1)}, bf16[256,128]{1,0:T(8,128)(2,1)}, bf16[256,128]{1,0:T(8,128)(2,1)}) custom-call(bf16[256,1024]{1,0:T(8,128)(2,1)S(1)} %get-tuple-element.6.query_grad, bf16[256,128]{1,0:T(8,128)(2,1)S(1)} %get-tuple-element.7.key_grad, bf16[256,128]{1,0:T(8,128)(2,1)S(1)} %get-tuple-element.8.value_grad), custom_call_target="tpu_custom_call" | custom-call | tf_op jit(solution)/shard_map/place_grads/pallas_call | solution.py:271
where the time goes:
time: 26.4 us; the launch traced here: 26.2 us
  Pallas kernels  25.6 us (97%)
  between operations  0.64 us (2%)
    pallas_call x1, Pallas kernels, local(): pl.pallas_call(functools.partial(kernel, n, heads, half, width), name='at...  24.7 us
    pallas_call x1, Pallas kernels, local(): pl.pallas_call(place, name='place_grads', out_shape=tuple((pltpu.HBM(g.sh...  0.85 us

commit v1 on v0

--- a/solution.py
+++ b/solution.py
@@ -28,16 +28,39 @@
     query_out, key_out, value_out,
     query, grad, norm, dot, keys, values, span,
     got, part, back, score_grads, own_key, own_value,
-    local_sem, span_sem, send_sem, recv_sem, part_send_sem, back_sem,
+    near_ready, far_ready, relay, local_sem, span_sem, send_sem, recv_sem, part_send_sem, back_sem,
 ):
     me = lax.axis_index("ctx")
     right, left = lax.rem(me + 1, n), lax.rem(me + n - 1, n)
     across = lax.rem(me + n // 2, n)
     inv_root = 1.0 / math.sqrt(width)
 
+    kind = lax.rem(me, 4)
     barrier = pltpu.get_barrier_semaphore()
-    for device in (right, left, across):
-        pl.semaphore_signal(barrier, inc=1, device_id={"ctx": device}, device_id_type=MESH)
+
+    def tell(sem, device):
+        pl.semaphore_signal(sem, inc=1, device_id={"ctx": device}, device_id_type=MESH)
+
+    @pl.when(kind == 0)
+    def _():
+        tell(barrier, left)
+        tell(barrier, across)
+
+    @pl.when(kind == 1)
+    def _():
+        tell(barrier, right)
+        tell(barrier, across)
+        tell(barrier, left)
+
+    @pl.when(kind == 2)
+    def _():
+        tell(barrier, right)
+        pl.semaphore_wait(barrier, 1)
+        tell(near_ready, left)
+
+    @pl.when(kind == 3)
+    def _():
+        tell(barrier, across)
 
     loads = []
     for source, target in ((key_hbm, keys), (value_hbm, values), (query_hbm, query), (grad_hbm, grad)):
@@ -56,9 +79,8 @@
     span_load.start()
 
     def offer(slot, block, which, device):
-        source = (key_hbm, value_hbm)[which].at[pl.ds(block * half, half)]
         return pltpu.make_async_remote_copy(
-            src_ref=source,
+            src_ref=(keys, values)[which].at[block],
             dst_ref=got.at[slot, block, which],
             send_sem=send_sem.at[slot, block, which],
             recv_sem=recv_sem.at[slot, block, which],
@@ -66,44 +88,70 @@
             device_id_type=MESH,
         )
 
-    pl.semaphore_wait(barrier, 3)
-    offers = {}
-    for block in range(2):
-        for slot, device in ((NEAR, right), (FAR, across)):
-            for which in range(2):
-                offers[slot, block, which] = offer(slot, block, which, device)
-                offers[slot, block, which].start()
-
-    for load in loads:
+    def near_offers():
+        for block in range(2):
+            for which in range(2):
+                offer(NEAR, block, which, right).start()
+
+    def far_offers():
+        for block in range(2):
+            for which in range(2):
+                offer(FAR, block, which, across).start()
+
+    @pl.when(kind != 2)
+    def _():
+        pl.semaphore_wait(barrier, jnp.where(kind == 0, 2, jnp.where(kind == 3, 3, 1)))
+
+    for load in loads[:4]:
+        load.wait()
+
+    @pl.when(kind == 0)
+    def _():
+        near_offers()
+        far_offers()
+
+    @pl.when(kind == 1)
+    def _():
+        far_offers()
+
+    @pl.when(kind == 2)
+    def _():
+        pl.semaphore_wait(far_ready, 1)
+        near_offers()
+        far_offers()
+
+    @pl.when(kind == 3)
+    def _():
+        tell(relay, across)
+        near_offers()
+        far_offers()
+        pl.semaphore_wait(relay, 1)
+        tell(far_ready, left)
+
+    for load in loads[4:]:
         load.wait()
     span_load.wait()
     own_span = span[me]
 
-    causal = lax.broadcasted_iota(jnp.int32, (half, 2 * half), 0) <= (
-        lax.broadcasted_iota(jnp.int32, (half, 2 * half), 1) % half
+    causal = lax.broadcasted_iota(jnp.int32, (half, heads * half), 0) <= (
+        lax.broadcasted_iota(jnp.int32, (half, heads * half), 1) % half
     )
 
+    def by_head(ref, at):
+        return jnp.concatenate([ref[at, :, pl.ds(h * width, width)] for h in range(heads)], axis=0)
+
+    def by_row(ref, at):
+        return jnp.concatenate([ref[at, pl.ds(h, 1), :] for h in range(heads)], axis=1)
+
     def block_grads(key_block, value_block, at, slot, diagonal):
-        key_term = value_term = None
-        for pair in range(heads // 2):
-            cols = [pl.ds((2 * pair + i) * width, width) for i in range(2)]
-            rows = [pl.ds(2 * pair + i, 1) for i in range(2)]
-            query_two = jnp.concatenate([query[at, :, c] for c in cols], axis=0)
-            grad_two = jnp.concatenate([grad[at, :, c] for c in cols], axis=0)
-            norm_two = jnp.concatenate([norm[at, r, :] for r in rows], axis=1)
-            dot_two = jnp.concatenate([dot[at, r, :] for r in rows], axis=1)
-            scores = dot_nt(key_block, query_two) * inv_root
-            weights = jnp.exp(scores - norm_two)
-            if diagonal:
-                weights = jnp.where(causal, weights, 0.0)
-            prob_grad = dot_nt(value_block, grad_two)
-            score_grad = (weights * (prob_grad - dot_two)).astype(BF16)
-            score_grads[slot, :, pl.ds(pair * 2 * half, 2 * half)] = score_grad
-            value_now = dot_nn(weights.astype(BF16), grad_two)
-            key_now = dot_nn(score_grad, query_two)
-            value_term = value_now if pair == 0 else value_term + value_now
-            key_term = key_now if pair == 0 else key_term + key_now
-        return key_term * inv_root, value_term
+        query_all, grad_all = by_head(query, at), by_head(grad, at)
+        weights = jnp.exp(dot_nt(key_block, query_all) * inv_root - by_row(norm, at))
+        if diagonal:
+            weights = jnp.where(causal, weights, 0.0)
+        score_grad = (weights * (dot_nt(value_block, grad_all) - by_row(dot, at))).astype(BF16)
+        score_grads[slot] = score_grad
+        value_term = dot_nn(weights.astype(BF16), grad_all)
+        return dot_nn(score_grad, query_all) * inv_root, value_term
 
     key_term, value_term = block_grads(keys[0], values[0], 0, OWN_EE, True)
     key_more, value_more = block_grads(keys[0], values[0], 1, OWN_LE, False)
@@ -111,10 +159,16 @@
     own_value[0] = value_term + value_more
     own_key[1], own_value[1] = block_grads(keys[1], values[1], 1, OWN_LL, True)
 
-    odd = lax.rem(me, 2)
+    far_first = jnp.where(kind == 0, 1, 0)
 
     def partner(step, _):
-        slot = lax.rem(step + 1 + odd, 2)
+        slot = lax.rem(step + far_first, 2)
+
+        @pl.when((kind == 1) & (step == 1))
+        def _():
+            pl.semaphore_wait(near_ready, 1)
+            near_offers()
+
         source = jnp.where(slot == NEAR, left, across)
         other_span = span[source]
         second = jnp.where(other_span < own_span, 0, 1)
@@ -187,23 +241,22 @@
                 pltpu.make_async_copy(
                     back.at[slot, turn, which], back.at[slot, turn, which], back_sem.at[slot, turn, which]
                 ).wait()
-    near_first = own_span < span[right]
-    far_first = own_span < span[across]
+    near_early_back = own_span < span[right]
+    far_early_back = own_span < span[across]
     for which, (own, out) in enumerate(((own_key, key_out), (own_value, value_out))):
         early = own[0] + back[NEAR, 0, which].astype(F32) + back[FAR, 0, which].astype(F32)
         late = own[1]
-        for slot, first in ((NEAR, near_first), (FAR, far_first)):
+        for slot, to_early in ((NEAR, near_early_back), (FAR, far_early_back)):
             term = back[slot, 1, which].astype(F32)
-            early = early + jnp.where(first, term, 0.0)
-            late = late + jnp.where(first, 0.0, term)
+            early = early + jnp.where(to_early, term, 0.0)
+            late = late + jnp.where(to_early, 0.0, term)
         out[pl.ds(0, half)] = early.astype(BF16)
         out[pl.ds(half, half)] = late.astype(BF16)
 
-    for key in offers:
-        offers[key].wait_send()
     for slot in (NEAR, FAR):
         for turn in range(2):
             for which in range(2):
+                offer(slot, turn, which, right if slot == NEAR else across).wait_send()
                 pltpu.make_async_copy(
                     part.at[slot, turn, which], part.at[slot, turn, which], part_send_sem.at[slot, turn, which]
                 ).wait()
@@ -254,6 +307,9 @@
             pltpu.VMEM((7, half, heads * half), BF16),
             pltpu.VMEM((2, half, width), F32),
             pltpu.VMEM((2, half, width), F32),
+            pltpu.SemaphoreType.REGULAR,
+            pltpu.SemaphoreType.REGULAR,
+            pltpu.SemaphoreType.REGULAR,
             pltpu.SemaphoreType.DMA((12,)),
             pltpu.SemaphoreType.DMA,
             pltpu.SemaphoreType.DMA((2, 2, 2)),

time: 26.4 us -> 24.9 us (0.943)
  the two profiles are of different devices: /device:TPU:64 before, /device:TPU:37 now
where the time goes in v1:
time: 24.9 us; the launch traced here: 24.8 us
  Pallas kernels  24.1 us (97%)
  between operations  0.64 us (3%)
    pallas_call x1, Pallas kernels, local(): pl.pallas_call(functools.partial(kernel, n, heads, half, width), name='at...  23.3 us
    pallas_call x1, Pallas kernels, local(): pl.pallas_call(place, name='place_grads', out_shape=tuple((pltpu.HBM(g.sh...  0.85 us

profile of v1, /device:TPU:37, one launch (start us, length us, event | category | flops | bytes accessed | tf_op | source)
XLA Modules:
  0.0 24.8 jit_solution(4469824501391878300)
XLA Ops:
  0.6 23.3 %attention_grads.1 = (bf16[256,1024]{1,0:T(8,128)(2,1)S(1)}, bf16[256,128]{1,0:T(8,128)(2,1)S(1)}, bf16[256,128]{1,0:T(8,128)(2,1)S(1)}) custom-call(bf16[256,1024]{1,0:T(8,128)(2,1)} %query_hbm.1, bf16[256,128]{1,0:T(8,128)(2,1)} %key_hbm.1, bf16[256,128]{1,0:T(8,128)(2,1)} %value_hbm.1, bf16[256,1024]{1,0:T(8,128)(2,1)} %grad_hbm.1, f32[8,256]{1,0:T(8,128)} %norm_hbm.1, ...), custom_call_target="tpu_custom_call" | custom-call | flops 1174405120 | bytes 2097152 | tf_op jit(solution)/shard_map/attention_grads/pallas_call | solution.py:286
  23.9 0.9 %place_grads.1 = (bf16[256,1024]{1,0:T(8,128)(2,1)}, bf16[256,128]{1,0:T(8,128)(2,1)}, bf16[256,128]{1,0:T(8,128)(2,1)}) custom-call(bf16[256,1024]{1,0:T(8,128)(2,1)S(1)} %get-tuple-element.6.query_grad, bf16[256,128]{1,0:T(8,128)(2,1)S(1)} %get-tuple-element.7.key_grad, bf16[256,128]{1,0:T(8,128)(2,1)S(1)} %get-tuple-element.8.value_grad), custom_call_target="tpu_custom_call" | custom-call | tf_op jit(solution)/shard_map/place_grads/pallas_call | solution.py:327

commit v2 on v1

v2 whole, which is shorter than its diff:
```python
import functools
import math

import jax
import jax.numpy as jnp
from jax import lax
from jax.experimental import pallas as pl
from jax.experimental.pallas import tpu as pltpu
from jax.sharding import PartitionSpec as P

MESH = pl.DeviceIdType.MESH
BF16, F32 = jnp.bfloat16, jnp.float32
NEAR, FAR = 0, 1
OWN_EE, OWN_LE, OWN_LL, PARTNER = 0, 1, 2, 3


def dot_nt(left, right):
    return lax.dot_general(left, right, (((1,), (1,)), ((), ())), preferred_element_type=F32)


def dot_nn(left, right):
    return jnp.dot(left, right, preferred_element_type=F32)


def kernel(
    n, heads, half, width,
    query_hbm, key_hbm, value_hbm, grad_hbm, norm_hbm, dot_hbm, span_hbm,
    query_out, key_out, value_out,
    query, grad, norm, dot, own, span,
    got, held, part, back, score_grads, own_key, own_value,
    near_ready, far_ready, relay, local_sem, span_sem, send_sem, recv_sem, held_sem, pass_sem, part_send_sem, back_sem,
):
    me = lax.axis_index("ctx")
    right, left = lax.rem(me + 1, n), lax.rem(me + n - 1, n)
    across = lax.rem(me + n // 2, n)
    inv_root = 1.0 / math.sqrt(width)

    kind = lax.rem(me, 4)
    lane, lanes = lax.axis_index("batch"), lax.axis_size("batch")
    low = lane < lanes // 2
    via = jnp.where(low, lane + lanes // 2, lanes - 1 - lane)
    giver = jnp.where(low, lanes - 1 - lane, lane - lanes // 2)
    barrier = pltpu.get_barrier_semaphore()

    def tell(sem, device, at=lane):
        pl.semaphore_signal(sem, inc=1, device_id={"ctx": device, "batch": at}, device_id_type=MESH)

    @pl.when(kind == 0)
    def _():
        tell(barrier, left)
        tell(barrier, across)

    @pl.when(kind == 1)
    def _():
        tell(barrier, lax.rem(me + 2, n), giver)
        tell(barrier, me, giver)
        tell(barrier, across)
        tell(barrier, left)

    @pl.when(kind == 2)
    def _():
        tell(barrier, right)
        tell(barrier, across)

    @pl.when(kind == 3)
    def _():
        tell(barrier, left)

    quarter = half // 2
    loads = []
    for which, source in enumerate((key_hbm, value_hbm)):
        loads.append((source, own.at[:, which]))
    for source, target in ((query_hbm, query), (grad_hbm, grad)):
        for block in range(2):
            loads.append((source.at[pl.ds(block * half, half)], target.at[block]))
    for source, target in ((norm_hbm, norm), (dot_hbm, dot)):
        for block in range(2):
            loads.append((source.at[:, pl.ds(block * half, half)], target.at[block]))
    loads = [
        pltpu.make_async_copy(source, target, local_sem.at[i])
        for i, (source, target) in enumerate(loads)
    ]
    span_load = pltpu.make_async_copy(span_hbm, span, span_sem)
    for load in loads[:2]:
        load.start()

    @pl.when(kind == 3)
    def _():
        pl.semaphore_wait(barrier, 3)
        tell(near_ready, lax.rem(me + n - 2, n), via)

    for load in loads[2:]:
        load.start()
    span_load.start()

    def offer(slot, piece, device):
        return pltpu.make_async_remote_copy(
            src_ref=own.at[piece],
            dst_ref=got.at[slot, piece],
            send_sem=send_sem.at[slot, piece],
            recv_sem=recv_sem.at[slot, piece],
            device_id={"ctx": device},
            device_id_type=MESH,
        )

    def hand(piece):
        return pltpu.make_async_remote_copy(
            src_ref=own.at[piece],
            dst_ref=held.at[piece],
            send_sem=send_sem.at[NEAR, piece],
            recv_sem=held_sem.at[piece],
            device_id={"ctx": me, "batch": via},
            device_id_type=MESH,
        )

    def pass_on(piece):
        return pltpu.make_async_remote_copy(
            src_ref=held.at[piece],
            dst_ref=got.at[NEAR, piece],
            send_sem=pass_sem.at[piece],
            recv_sem=recv_sem.at[NEAR, piece],
            device_id={"ctx": right, "batch": giver},
            device_id_type=MESH,
        )

    def near_offers():
        for piece in range(4):
            offer(NEAR, piece, right).start()

    def far_offers():
        for piece in range(4):
            offer(FAR, piece, across).start()

    @pl.when(kind != 3)
    def _():
        pl.semaphore_wait(barrier, 2)

    for load in loads[:2]:
        load.wait()

    @pl.when(kind == 1)
    def _():
        for piece in range(4):
            hand(piece).start()

    @pl.when(kind != 1)
    def _():
        near_offers()

    @pl.when(kind == 3)
    def _():
        pl.semaphore_wait(far_ready, 1)

    far_offers()

    @pl.when(kind == 2)
    def _():
        tell(relay, across)
        pl.semaphore_wait(relay, 1)
        tell(far_ready, right)

    for load in loads[2:]:
        load.wait()
    span_load.wait()
    own_span = span[me]

    causal = lax.broadcasted_iota(jnp.int32, (half, heads * half), 0) <= (
        lax.broadcasted_iota(jnp.int32, (half, heads * half), 1) % half
    )

    def by_head(ref, at):
        return jnp.concatenate([ref[at, :, pl.ds(h * width, width)] for h in range(heads)], axis=0)

    def by_row(ref, at):
        return jnp.concatenate([ref[at, pl.ds(h, 1), :] for h in range(heads)], axis=1)

    def block_grads(key_block, value_block, at, score_out, diagonal=False):
        query_all, grad_all = by_head(query, at), by_head(grad, at)
        weights = jnp.exp(dot_nt(key_block, query_all) * inv_root - by_row(norm, at))
        if diagonal:
            weights = jnp.where(causal, weights, 0.0)
        score_grad = (weights * (dot_nt(value_block, grad_all) - by_row(dot, at))).astype(BF16)
        score_out[...] = score_grad
        value_term = dot_nn(weights.astype(BF16), grad_all)
        return dot_nn(score_grad, query_all) * inv_root, value_term

    def joined(*pieces):
        return jnp.concatenate(pieces, axis=0)

    own_keys = [joined(own[2 * block, 0], own[2 * block + 1, 0]) for block in range(2)]
    own_values = [joined(own[2 * block, 1], own[2 * block + 1, 1]) for block in range(2)]
    key_term, value_term = block_grads(own_keys[0], own_values[0], 0, score_grads.at[OWN_EE], True)
    key_more, value_more = block_grads(own_keys[0], own_values[0], 1, score_grads.at[OWN_LE])
    own_key[0] = key_term + key_more
    own_value[0] = value_term + value_more
    own_key[1], own_value[1] = block_grads(own_keys[1], own_values[1], 1, score_grads.at[OWN_LL], True)

    far_first = jnp.where(kind == 0, 1, 0)

    def partner(step, _):
        slot = lax.rem(step + far_first, 2)

        @pl.when((kind == 1) & (step == 1))
        def _():
            pl.semaphore_wait(near_ready, 1)
            for piece in range(4):
                hand(piece).wait_recv()
                pass_on(piece).start()

        source = jnp.where(slot == NEAR, left, across)
        other_span = span[source]
        second = jnp.where(other_span < own_span, 0, 1)

        def give(first, count):
            pieces = pl.ds(first, count)
            return pltpu.make_async_remote_copy(
                src_ref=part.at[slot, pieces],
                dst_ref=back.at[slot, pieces],
                send_sem=part_send_sem.at[slot, first],
                recv_sem=back_sem.at[slot, first],
                device_id={"ctx": source},
                device_id_type=MESH,
            )

        def arrive(piece):
            pltpu.make_async_copy(got.at[slot, piece], got.at[slot, piece], recv_sem.at[slot, piece]).wait()

        arrive(0)
        arrive(1)
        score_slot = PARTNER + 2 * slot
        key_term, value_term = block_grads(
            joined(got[slot, 0, 0], got[slot, 1, 0]),
            joined(got[slot, 0, 1], got[slot, 1, 1]),
            1,
            score_grads.at[score_slot],
        )
        for piece in range(2):
            rows = slice(piece * quarter, (piece + 1) * quarter)
            part[slot, piece, 0] = key_term[rows].astype(BF16)
            part[slot, piece, 1] = value_term[rows].astype(BF16)
        give(0, 2).start()

        for piece in range(2):
            arrive(2 + piece)
            key_block, value_block = (
                jnp.where(second == 0, got[slot, piece, which], got[slot, 2 + piece, which]) for which in range(2)
            )
            key_term, value_term = block_grads(
                key_block, value_block, second, score_grads.at[score_slot + 1, pl.ds(piece * quarter, quarter)]
            )
            part[slot, 2 + piece, 0] = key_term.astype(BF16)
            part[slot, 2 + piece, 1] = value_term.astype(BF16)
            give(2 + piece, 1).start()
        return 0

    lax.fori_loop(0, 2, partner, 0)

    near_early = span[left] < own_span
    far_early = span[across] < own_span

    def first_keys(slot):
        return joined(got[slot, 0, 0], got[slot, 1, 0])

    def second_keys(slot, early):
        return jnp.where(early, first_keys(slot), joined(got[slot, 2, 0], got[slot, 3, 0]))

    zero = jnp.zeros((half, width), BF16)
    near_second, far_second = second_keys(NEAR, near_early), second_keys(FAR, far_early)
    near_slot, far_slot = PARTNER + 2 * NEAR, PARTNER + 2 * FAR
    early_keys = joined(
        own_keys[0], jnp.where(near_early, near_second, zero), jnp.where(far_early, far_second, zero)
    ).T
    late_keys = joined(
        own_keys[0], own_keys[1], first_keys(NEAR), first_keys(FAR),
        jnp.where(near_early, zero, near_second), jnp.where(far_early, zero, far_second),
    ).T
    early_slots = (OWN_EE, near_slot + 1, far_slot + 1)
    late_slots = (OWN_LE, OWN_LL, near_slot, far_slot, near_slot + 1, far_slot + 1)
    stores = []
    for pair in range(heads // 2):
        cols = pl.ds(pair * 2 * half, 2 * half)
        for block, (key_side, slots) in enumerate(((early_keys, early_slots), (late_keys, late_slots))):
            scores = jnp.concatenate([score_grads[s, :, cols] for s in slots], axis=0)
            turned = (dot_nn(key_side, scores) * inv_root).astype(BF16)
            for i in range(2):
                query_out[pl.ds(block * half, half), pl.ds((2 * pair + i) * width, width)] = (
                    turned[:, i * half : (i + 1) * half].T
                )

    pieces_back = ((0, 2), (2, 1), (3, 1))
    for slot in (NEAR, FAR):
        for first, count in pieces_back:
            arrived = back.at[slot, pl.ds(first, count)]
            pltpu.make_async_copy(arrived, arrived, back_sem.at[slot, first]).wait()
    near_early_back = own_span < span[right]
    far_early_back = own_span < span[across]
    for which, (sums, out) in enumerate(((own_key, key_out), (own_value, value_out))):
        early, late = sums[0], sums[1]
        for slot, to_early in ((NEAR, near_early_back), (FAR, far_early_back)):
            term = joined(back[slot, 2, which], back[slot, 3, which]).astype(F32)
            early = early + joined(back[slot, 0, which], back[slot, 1, which]).astype(F32)
            early = early + jnp.where(to_early, term, 0.0)
            late = late + jnp.where(to_early, 0.0, term)
        out[pl.ds(0, half)] = early.astype(BF16)
        out[pl.ds(half, half)] = late.astype(BF16)

    for slot in (NEAR, FAR):
        for piece in range(4):
            offer(slot, piece, right if slot == NEAR else across).wait_send()
        for first, count in pieces_back:
            sent = part.at[slot, pl.ds(first, count)]
            pltpu.make_async_copy(sent, sent, part_send_sem.at[slot, first]).wait()

    @pl.when(kind == 1)
    def _():
        for piece in range(4):
            pass_on(piece).wait_send()


def place(query_grad, key_grad, value_grad, query_out, key_out, value_out, sem):
    copies = [
        pltpu.make_async_copy(source, target, sem.at[i])
        for i, (source, target) in enumerate(
            ((query_grad, query_out), (key_grad, key_out), (value_grad, value_out))
        )
    ]
    for copy in copies:
        copy.start()
    for copy in copies:
        copy.wait()


def local(query_rows, key_rows, value_rows, out_grad, log_norm, row_dot, span_order):
    n = lax.axis_size("ctx")
    rows, width = key_rows.shape
    heads, half = log_norm.shape[0], rows // 2
    hbm = pl.BlockSpec(memory_space=pltpu.HBM)
    vmem = pl.BlockSpec(memory_space=pltpu.VMEM)
    blocks = 8 * 3 * half * half * heads * 7
    key_pieces, value_pieces = (x.reshape(4, half // 2, width) for x in (key_rows, value_rows))
    args = (query_rows, key_pieces, value_pieces, out_grad, log_norm, row_dot, span_order)
    grads = pl.pallas_call(
        functools.partial(kernel, n, heads, half, width),
        name="attention_grads",
        out_shape=(
            pltpu.VMEM(query_rows.shape, BF16),
            pltpu.VMEM(key_rows.shape, BF16),
            pltpu.VMEM(value_rows.shape, BF16),
        ),
        in_specs=[hbm] * 7,
        out_specs=(vmem, vmem, vmem),
        scratch_shapes=[
            pltpu.VMEM((2, half, heads * width), BF16),
            pltpu.VMEM((2, half, heads * width), BF16),
            pltpu.VMEM((2, heads, half), F32),
            pltpu.VMEM((2, heads, half), F32),
            pltpu.VMEM((4, 2, half // 2, width), BF16),
            pltpu.SMEM((n,), jnp.int32),
            pltpu.VMEM((2, 4, 2, half // 2, width), BF16),
            pltpu.VMEM((4, 2, half // 2, width), BF16),
            pltpu.VMEM((2, 4, 2, half // 2, width), BF16),
            pltpu.VMEM((2, 4, 2, half // 2, width), BF16),
            pltpu.VMEM((7, half, heads * half), BF16),
            pltpu.VMEM((2, half, width), F32),
            pltpu.VMEM((2, half, width), F32),
            pltpu.SemaphoreType.REGULAR,
            pltpu.SemaphoreType.REGULAR,
            pltpu.SemaphoreType.REGULAR,
            pltpu.SemaphoreType.DMA((10,)),
            pltpu.SemaphoreType.DMA,
            pltpu.SemaphoreType.DMA((2, 4)),
            pltpu.SemaphoreType.DMA((2, 4)),
            pltpu.SemaphoreType.DMA((4,)),
            pltpu.SemaphoreType.DMA((4,)),
            pltpu.SemaphoreType.DMA((2, 4)),
            pltpu.SemaphoreType.DMA((2, 4)),
        ],
        compiler_params=pltpu.CompilerParams(
            collective_id=0, has_side_effects=True, vmem_limit_bytes=24 * 1024 * 1024
        ),
        cost_estimate=pl.CostEstimate(
            flops=10 * half * half * width * heads * 7, bytes_accessed=2 << 20, transcendentals=blocks // 24
        ),
    )(*[pltpu.with_memory_space_constraint(x, pltpu.HBM) for x in args])
    return pl.pallas_call(
        place,
        name="place_grads",
        out_shape=tuple(pltpu.HBM(g.shape, g.dtype) for g in grads),
        in_specs=[vmem] * 3,
        out_specs=(hbm,) * 3,
        scratch_shapes=[pltpu.SemaphoreType.DMA((3,))],
    )(*[pltpu.with_memory_space_constraint(g, pltpu.VMEM) for g in grads])


def solution(mesh):
    return jax.shard_map(
        local,
        mesh=mesh,
        in_specs=(
            P(("batch", "ctx"), None),
            P(("batch", "ctx"), None),
            P(("batch", "ctx"), None),
            P(("batch", "ctx"), None),
            P(None, ("batch", "ctx")),
            P(None, ("batch", "ctx")),
            P("batch"),
        ),
        out_specs=(P(("batch", "ctx"), None), P(("batch", "ctx"), None), P(("batch", "ctx"), None)),
        check_vma=False,
    )
```

time: 24.9 us -> 23.3 us (0.936)
  the two profiles are of different devices: /device:TPU:37 before, /device:TPU:121 now
where the time goes in v2:
time: 23.3 us; the launch traced here: 23.2 us
  Pallas kernels  22.5 us (97%)
  between operations  0.64 us (3%)
    pallas_call x1, Pallas kernels, local(): pl.pallas_call(functools.partial(kernel, n, heads, half, width), name='at...  21.7 us
    pallas_call x1, Pallas kernels, local(): pl.pallas_call(place, name='place_grads', out_shape=tuple((pltpu.HBM(g.sh...  0.85 us

profile of v2, /device:TPU:121, one launch (start us, length us, event | category | flops | bytes accessed | tf_op | source)
XLA Modules:
  0.0 23.2 jit_solution(15102492031807861921)
XLA Ops:
  0.6 21.7 %attention_grads.1 = (bf16[256,1024]{1,0:T(8,128)(2,1)S(1)}, bf16[256,128]{1,0:T(8,128)(2,1)S(1)}, bf16[256,128]{1,0:T(8,128)(2,1)S(1)}) custom-call(bf16[256,1024]{1,0:T(8,128)(2,1)} %query_hbm.1, bf16[4,64,128]{2,1,0:T(8,128)(2,1)} %bitcast.2, bf16[4,64,128]{2,1,0:T(8,128)(2,1)} %bitcast.3, bf16[256,1024]{1,0:T(8,128)(2,1)} %grad_hbm.1, ...), custom_call_target="tpu_custom_call" | custom-call | flops 1174405120 | bytes 2097152 | tf_op jit(solution)/shard_map/attention_grads/pallas_call | solution.py:342
  22.3 0.9 %place_grads.1 = (bf16[256,1024]{1,0:T(8,128)(2,1)}, bf16[256,128]{1,0:T(8,128)(2,1)}, bf16[256,128]{1,0:T(8,128)(2,1)}) custom-call(bf16[256,1024]{1,0:T(8,128)(2,1)S(1)} %get-tuple-element.6.query_grad, bf16[256,128]{1,0:T(8,128)(2,1)S(1)} %get-tuple-element.7.key_grad, bf16[256,128]{1,0:T(8,128)(2,1)S(1)} %get-tuple-element.8.value_grad), custom_call_target="tpu_custom_call" | custom-call | tf_op jit(solution)/shard_map/place_grads/pallas_call | solution.py:385

commit v3 on v2

v3 whole, which is shorter than its diff:
```python
import functools
import math

import jax
import jax.numpy as jnp
from jax import lax
from jax.experimental import pallas as pl
from jax.experimental.pallas import tpu as pltpu
from jax.sharding import PartitionSpec as P

MESH = pl.DeviceIdType.MESH
BF16, F32 = jnp.bfloat16, jnp.float32
NEAR, FAR = 0, 1
OWN_EE, OWN_LE, OWN_LL, PARTNER = 0, 1, 2, 3
CHUNKS = 8
PIECES = ((0, 4), (4, 3), (7, 1))


def dot_nt(left, right):
    return lax.dot_general(left, right, (((1,), (1,)), ((), ())), preferred_element_type=F32)


def dot_nn(left, right):
    return jnp.dot(left, right, preferred_element_type=F32)


def kernel(
    n, heads, half, width,
    query_hbm, key_hbm, value_hbm, grad_hbm, norm_hbm, dot_hbm, span_hbm,
    query_out, key_out, value_out,
    sides, rows, own, span,
    got, held, part, back, score_grads, own_key, own_value,
    ready, load_sem, span_sem, send_sem, recv_sem, held_sem, pass_sem, part_send_sem, back_sem,
):
    me = lax.axis_index("ctx")
    right, left = lax.rem(me + 1, n), lax.rem(me + n - 1, n)
    across = lax.rem(me + n // 2, n)
    inv_root = 1.0 / math.sqrt(width)

    kind = lax.rem(me, 4)
    lane, lanes = lax.axis_index("batch"), lax.axis_size("batch")
    low = lane < lanes // 2
    via = jnp.where(low, lane + lanes // 2, lanes - 1 - lane)
    giver = jnp.where(low, lanes - 1 - lane, lane - lanes // 2)
    barrier = pltpu.get_barrier_semaphore()

    def tell(sem, device, at=lane):
        pl.semaphore_signal(sem, inc=1, device_id={"ctx": device, "batch": at}, device_id_type=MESH)

    @pl.when(kind == 0)
    def _():
        tell(barrier, left)
        tell(barrier, across)

    @pl.when(kind == 1)
    def _():
        tell(barrier, lax.rem(me + 2, n), giver)
        tell(barrier, me, giver)
        tell(barrier, across)
        tell(barrier, left)

    @pl.when(kind == 2)
    def _():
        tell(barrier, right)
        tell(barrier, across)

    @pl.when(kind == 3)
    def _():
        tell(barrier, left)

    chunk = 2 * half // CHUNKS
    query, grad, norm, dot = sides.at[0], sides.at[1], rows.at[0], rows.at[1]

    def load(source, target, group):
        pltpu.make_async_copy(source, target, load_sem.at[group]).start()

    def wait_all(ref, sem):
        pltpu.make_async_copy(ref, ref, sem).wait()

    for which, source in enumerate((key_hbm, value_hbm)):
        load(source, own.at[:, which], 0)

    def near_from_hbm():
        for piece, (first, count) in enumerate(PIECES):
            for which, source in enumerate((key_hbm, value_hbm)):
                pltpu.make_async_remote_copy(
                    src_ref=source.at[pl.ds(first, count)],
                    dst_ref=got.at[NEAR, pl.ds(first, count), which],
                    send_sem=send_sem,
                    recv_sem=recv_sem.at[NEAR, piece],
                    device_id={"ctx": right},
                    device_id_type=MESH,
                ).start()

    @pl.when(kind == 3)
    def _():
        pl.semaphore_wait(barrier, 3)
        tell(ready, lax.rem(me + n - 2, n), via)
        near_from_hbm()

    for which, source in enumerate((query_hbm, grad_hbm)):
        for block in range(2):
            load(source.at[pl.ds(block * half, half)], sides.at[which, block], 1)
    for which, source in enumerate((norm_hbm, dot_hbm)):
        for block in range(2):
            load(source.at[:, pl.ds(block * half, half)], rows.at[which, block], 2)
    span_load = pltpu.make_async_copy(span_hbm, span, span_sem)
    span_load.start()

    def offer(slot, piece, device):
        return pltpu.make_async_remote_copy(
            src_ref=own.at[pl.ds(*PIECES[piece])],
            dst_ref=got.at[slot, pl.ds(*PIECES[piece])],
            send_sem=send_sem,
            recv_sem=recv_sem.at[slot, piece],
            device_id={"ctx": device},
            device_id_type=MESH,
        )

    def hand():
        return pltpu.make_async_remote_copy(
            src_ref=own,
            dst_ref=held,
            send_sem=send_sem,
            recv_sem=held_sem,
            device_id={"ctx": me, "batch": via},
            device_id_type=MESH,
        )

    def pass_on(piece):
        return pltpu.make_async_remote_copy(
            src_ref=held.at[pl.ds(*PIECES[piece])],
            dst_ref=got.at[NEAR, pl.ds(*PIECES[piece])],
            send_sem=pass_sem,
            recv_sem=recv_sem.at[NEAR, piece],
            device_id={"ctx": right, "batch": giver},
            device_id_type=MESH,
        )

    def near_offers():
        for piece in range(len(PIECES)):
            offer(NEAR, piece, right).start()

    def far_offers():
        for piece in range(len(PIECES)):
            offer(FAR, piece, across).start()

    @pl.when(kind != 3)
    def _():
        pl.semaphore_wait(barrier, 2)

    wait_all(own, load_sem.at[0])

    @pl.when(kind == 1)
    def _():
        hand().start()

    @pl.when((kind == 0) | (kind == 2))
    def _():
        near_offers()

    @pl.when(kind == 3)
    def _():
        pl.semaphore_wait(ready, 1)

    far_offers()

    @pl.when(kind == 2)
    def _():
        tell(ready, across)
        pl.semaphore_wait(ready, 1)
        tell(ready, right)

    wait_all(sides, load_sem.at[1])
    wait_all(rows, load_sem.at[2])
    span_load.wait()
    own_span = span[me]

    causal = lax.broadcasted_iota(jnp.int32, (half, heads * half), 0) <= (
        lax.broadcasted_iota(jnp.int32, (half, heads * half), 1) % half
    )

    def by_head(ref, at):
        return jnp.concatenate([ref[at, :, pl.ds(h * width, width)] for h in range(heads)], axis=0)

    def by_row(ref, at):
        return jnp.concatenate([ref[at, pl.ds(h, 1), :] for h in range(heads)], axis=1)

    def block_grads(key_block, value_block, at, score_out, diagonal=False):
        query_all, grad_all = by_head(query, at), by_head(grad, at)
        weights = jnp.exp(dot_nt(key_block, query_all) * inv_root - by_row(norm, at))
        if diagonal:
            weights = jnp.where(causal, weights, 0.0)
        score_grad = (weights * (dot_nt(value_block, grad_all) - by_row(dot, at))).astype(BF16)
        score_out[...] = score_grad
        value_term = dot_nn(weights.astype(BF16), grad_all)
        return dot_nn(score_grad, query_all) * inv_root, value_term

    def joined(*pieces):
        return jnp.concatenate(pieces, axis=0)

    def block_of(ref, block, which, slot=()):
        chunks = range(block * CHUNKS // 2, (block + 1) * CHUNKS // 2)
        return joined(*(ref[(*slot, c, which)] for c in chunks))

    own_keys = [block_of(own, block, 0) for block in range(2)]
    own_values = [block_of(own, block, 1) for block in range(2)]
    key_term, value_term = block_grads(own_keys[0], own_values[0], 0, score_grads.at[OWN_EE], True)
    key_more, value_more = block_grads(own_keys[0], own_values[0], 1, score_grads.at[OWN_LE])
    own_key[0] = key_term + key_more
    own_value[0] = value_term + value_more
    own_key[1], own_value[1] = block_grads(own_keys[1], own_values[1], 1, score_grads.at[OWN_LL], True)

    far_first = jnp.where(kind == 0, 1, 0)

    def partner(step, _):
        slot = lax.rem(step + far_first, 2)

        @pl.when((kind == 1) & (step == 1))
        def _():
            pl.semaphore_wait(ready, 1)
            hand().wait_recv()
            for piece in range(len(PIECES)):
                pass_on(piece).start()

        source = jnp.where(slot == NEAR, left, across)
        other_span = span[source]
        second = jnp.where(other_span < own_span, 0, 1)

        def give(piece):
            chunks = pl.ds(*PIECES[piece])
            return pltpu.make_async_remote_copy(
                src_ref=part.at[slot, chunks],
                dst_ref=back.at[slot, chunks],
                send_sem=part_send_sem,
                recv_sem=back_sem.at[slot],
                device_id={"ctx": source},
                device_id_type=MESH,
            )

        for piece, (first, count) in enumerate(PIECES):
            wait_all(got.at[slot, pl.ds(first, count)], recv_sem.at[slot, piece])
            chunks = range(first, first + count)
            block, before = divmod(first, CHUNKS // 2)
            if block == 0:
                at = 1
                blocks = [joined(*(got[slot, c, which] for c in chunks)) for which in range(2)]
            else:
                at = second
                blocks = [
                    joined(*(
                        jnp.where(second == 0, got[slot, c - CHUNKS // 2, which], got[slot, c, which]) for c in chunks
                    ))
                    for which in range(2)
                ]
            score_out = score_grads.at[PARTNER + 2 * slot + block, pl.ds(before * chunk, count * chunk)]
            terms = block_grads(*blocks, at, score_out)
            for which in range(2):
                for i, c in enumerate(chunks):
                    part[slot, c, which] = terms[which][i * chunk : (i + 1) * chunk].astype(BF16)
            give(piece).start()
        return 0

    lax.fori_loop(0, 2, partner, 0)

    near_early = span[left] < own_span
    far_early = span[across] < own_span

    def first_keys(slot):
        return block_of(got, 0, 0, (slot,))

    def second_keys(slot, early):
        return jnp.where(early, first_keys(slot), block_of(got, 1, 0, (slot,)))

    zero = jnp.zeros((half, width), BF16)
    near_second, far_second = second_keys(NEAR, near_early), second_keys(FAR, far_early)
    near_slot, far_slot = PARTNER + 2 * NEAR, PARTNER + 2 * FAR
    early_keys = joined(
        own_keys[0], jnp.where(near_early, near_second, zero), jnp.where(far_early, far_second, zero)
    ).T
    late_keys = joined(
        own_keys[0], own_keys[1], first_keys(NEAR), first_keys(FAR),
        jnp.where(near_early, zero, near_second), jnp.where(far_early, zero, far_second),
    ).T
    early_slots = (OWN_EE, near_slot + 1, far_slot + 1)
    late_slots = (OWN_LE, OWN_LL, near_slot, far_slot, near_slot + 1, far_slot + 1)
    stores = []
    for pair in range(heads // 2):
        cols = pl.ds(pair * 2 * half, 2 * half)
        for block, (key_side, slots) in enumerate(((early_keys, early_slots), (late_keys, late_slots))):
            scores = jnp.concatenate([score_grads[s, :, cols] for s in slots], axis=0)
            turned = (dot_nn(key_side, scores) * inv_root).astype(BF16)
            for i in range(2):
                query_out[pl.ds(block * half, half), pl.ds((2 * pair + i) * width, width)] = (
                    turned[:, i * half : (i + 1) * half].T
                )

    wait_all(got, send_sem)
    wait_all(part, part_send_sem)

    @pl.when(kind == 1)
    def _():
        wait_all(held, pass_sem)

    for slot in (FAR, NEAR):
        wait_all(back.at[slot], back_sem.at[slot])
    near_early_back = own_span < span[right]
    far_early_back = own_span < span[across]
    for which, (sums, out) in enumerate(((own_key, key_out), (own_value, value_out))):
        early, late = sums[0], sums[1]
        for slot, to_early in ((NEAR, near_early_back), (FAR, far_early_back)):
            term = block_of(back, 1, which, (slot,)).astype(F32)
            early = early + block_of(back, 0, which, (slot,)).astype(F32)
            early = early + jnp.where(to_early, term, 0.0)
            late = late + jnp.where(to_early, 0.0, term)
        out[pl.ds(0, half)] = early.astype(BF16)
        out[pl.ds(half, half)] = late.astype(BF16)


def place(query_grad, key_grad, value_grad, query_out, key_out, value_out, sem):
    copies = [
        pltpu.make_async_copy(source, target, sem.at[i])
        for i, (source, target) in enumerate(
            ((query_grad, query_out), (key_grad, key_out), (value_grad, value_out))
        )
    ]
    for copy in copies:
        copy.start()
    for copy in copies:
        copy.wait()


def local(query_rows, key_rows, value_rows, out_grad, log_norm, row_dot, span_order):
    n = lax.axis_size("ctx")
    rows, width = key_rows.shape
    heads, half = log_norm.shape[0], rows // 2
    hbm = pl.BlockSpec(memory_space=pltpu.HBM)
    vmem = pl.BlockSpec(memory_space=pltpu.VMEM)
    blocks = 8 * 3 * half * half * heads * 7
    key_pieces, value_pieces = (x.reshape(CHUNKS, rows // CHUNKS, width) for x in (key_rows, value_rows))
    args = (query_rows, key_pieces, value_pieces, out_grad, log_norm, row_dot, span_order)
    grads = pl.pallas_call(
        functools.partial(kernel, n, heads, half, width),
        name="attention_grads",
        out_shape=(
            pltpu.VMEM(query_rows.shape, BF16),
            pltpu.VMEM(key_rows.shape, BF16),
            pltpu.VMEM(value_rows.shape, BF16),
        ),
        in_specs=[hbm] * 7,
        out_specs=(vmem, vmem, vmem),
        scratch_shapes=[
            pltpu.VMEM((2, 2, half, heads * width), BF16),
            pltpu.VMEM((2, 2, heads, half), F32),
            pltpu.VMEM((CHUNKS, 2, rows // CHUNKS, width), BF16),
            pltpu.SMEM((n,), jnp.int32),
            pltpu.VMEM((2, CHUNKS, 2, rows // CHUNKS, width), BF16),
            pltpu.VMEM((CHUNKS, 2, rows // CHUNKS, width), BF16),
            pltpu.VMEM((2, CHUNKS, 2, rows // CHUNKS, width), BF16),
            pltpu.VMEM((2, CHUNKS, 2, rows // CHUNKS, width), BF16),
            pltpu.VMEM((7, half, heads * half), BF16),
            pltpu.VMEM((2, half, width), F32),
            pltpu.VMEM((2, half, width), F32),
            pltpu.SemaphoreType.REGULAR,
            pltpu.SemaphoreType.DMA((3,)),
            pltpu.SemaphoreType.DMA,
            pltpu.SemaphoreType.DMA,
            pltpu.SemaphoreType.DMA((2, len(PIECES))),
            pltpu.SemaphoreType.DMA,
            pltpu.SemaphoreType.DMA,
            pltpu.SemaphoreType.DMA,
            pltpu.SemaphoreType.DMA((2,)),
        ],
        compiler_params=pltpu.CompilerParams(
            collective_id=0, has_side_effects=True, vmem_limit_bytes=24 * 1024 * 1024
        ),
        cost_estimate=pl.CostEstimate(
            flops=10 * half * half * width * heads * 7, bytes_accessed=2 << 20, transcendentals=blocks // 24
        ),
    )(*[pltpu.with_memory_space_constraint(x, pltpu.HBM) for x in args])
    return pl.pallas_call(
        place,
        name="place_grads",
        out_shape=tuple(pltpu.HBM(g.shape, g.dtype) for g in grads),
        in_specs=[vmem] * 3,
        out_specs=(hbm,) * 3,
        scratch_shapes=[pltpu.SemaphoreType.DMA((3,))],
    )(*[pltpu.with_memory_space_constraint(g, pltpu.VMEM) for g in grads])


def solution(mesh):
    return jax.shard_map(
        local,
        mesh=mesh,
        in_specs=(
            P(("batch", "ctx"), None),
            P(("batch", "ctx"), None),
            P(("batch", "ctx"), None),
            P(("batch", "ctx"), None),
            P(None, ("batch", "ctx")),
            P(None, ("batch", "ctx")),
            P("batch"),
        ),
        out_specs=(P(("batch", "ctx"), None), P(("batch", "ctx"), None), P(("batch", "ctx"), None)),
        check_vma=False,
    )
```

time: 23.3 us -> 23 us (0.987)
  the two profiles are of different devices: /device:TPU:121 before, /device:TPU:127 now
where the time goes in v3:
time: 23 us; the launch traced here: 22.9 us
  Pallas kernels  22.2 us (97%)
  between operations  0.64 us (3%)
    pallas_call x1, Pallas kernels, local(): pl.pallas_call(functools.partial(kernel, n, heads, half, width), name='at...  21.4 us
    pallas_call x1, Pallas kernels, local(): pl.pallas_call(place, name='place_grads', out_shape=tuple((pltpu.HBM(g.sh...  0.85 us

profile of v3, /device:TPU:127, one launch (start us, length us, event | category | flops | bytes accessed | tf_op | source)
XLA Modules:
  0.0 22.9 jit_solution(17205263837433149202)
XLA Ops:
  0.6 21.4 %attention_grads.1 = (bf16[256,1024]{1,0:T(8,128)(2,1)S(1)}, bf16[256,128]{1,0:T(8,128)(2,1)S(1)}, bf16[256,128]{1,0:T(8,128)(2,1)S(1)}) custom-call(bf16[256,1024]{1,0:T(8,128)(2,1)} %query_hbm.1, bf16[8,32,128]{2,1,0:T(8,128)(2,1)} %bitcast.2, bf16[8,32,128]{2,1,0:T(8,128)(2,1)} %bitcast.3, bf16[256,1024]{1,0:T(8,128)(2,1)} %grad_hbm.1, ...), custom_call_target="tpu_custom_call" | custom-call | flops 1174405120 | bytes 2097152 | tf_op jit(solution)/shard_map/attention_grads/pallas_call | solution.py:342
  22.0 0.9 %place_grads.1 = (bf16[256,1024]{1,0:T(8,128)(2,1)}, bf16[256,128]{1,0:T(8,128)(2,1)}, bf16[256,128]{1,0:T(8,128)(2,1)}) custom-call(bf16[256,1024]{1,0:T(8,128)(2,1)S(1)} %get-tuple-element.6.query_grad, bf16[256,128]{1,0:T(8,128)(2,1)S(1)} %get-tuple-element.7.key_grad, bf16[256,128]{1,0:T(8,128)(2,1)S(1)} %get-tuple-element.8.value_grad), custom_call_target="tpu_custom_call" | custom-call | tf_op jit(solution)/shard_map/place_grads/pallas_call | solution.py:381

commit v4 on v3

--- a/solution.py
+++ b/solution.py
@@ -13,7 +13,7 @@
 NEAR, FAR = 0, 1
 OWN_EE, OWN_LE, OWN_LL, PARTNER = 0, 1, 2, 3
 CHUNKS = 8
-PIECES = ((0, 4), (4, 3), (7, 1))
+PIECES = ((0, 4), (4, 4))
 
 
 def dot_nt(left, right):
@@ -47,6 +47,11 @@
     def tell(sem, device, at=lane):
         pl.semaphore_signal(sem, inc=1, device_id={"ctx": device, "batch": at}, device_id_type=MESH)
 
+    @pl.when(kind == 2)
+    def _():
+        tell(barrier, right)
+        tell(barrier, across)
+
     @pl.when(kind == 0)
     def _():
         tell(barrier, left)
@@ -58,11 +63,6 @@
         tell(barrier, me, giver)
         tell(barrier, across)
         tell(barrier, left)
-
-    @pl.when(kind == 2)
-    def _():
-        tell(barrier, right)
-        tell(barrier, across)
 
     @pl.when(kind == 3)
     def _():
@@ -302,17 +302,17 @@
     def _():
         wait_all(held, pass_sem)
 
-    for slot in (FAR, NEAR):
-        wait_all(back.at[slot], back_sem.at[slot])
-    near_early_back = own_span < span[right]
-    far_early_back = own_span < span[across]
+    def add_returned(slot, early_back, which, early, late):
+        term = block_of(back, 1, which, (slot,)).astype(F32)
+        early = early + block_of(back, 0, which, (slot,)).astype(F32)
+        return early + jnp.where(early_back, term, 0.0), late + jnp.where(early_back, 0.0, term)
+
+    wait_all(back.at[FAR], back_sem.at[FAR])
+    for which, sums in enumerate((own_key, own_value)):
+        sums[0], sums[1] = add_returned(FAR, own_span < span[across], which, sums[0], sums[1])
+    wait_all(back.at[NEAR], back_sem.at[NEAR])
     for which, (sums, out) in enumerate(((own_key, key_out), (own_value, value_out))):
-        early, late = sums[0], sums[1]
-        for slot, to_early in ((NEAR, near_early_back), (FAR, far_early_back)):
-            term = block_of(back, 1, which, (slot,)).astype(F32)
-            early = early + block_of(back, 0, which, (slot,)).astype(F32)
-            early = early + jnp.where(to_early, term, 0.0)
-            late = late + jnp.where(to_early, 0.0, term)
+        early, late = add_returned(NEAR, own_span < span[right], which, sums[0], sums[1])
         out[pl.ds(0, half)] = early.astype(BF16)
         out[pl.ds(half, half)] = late.astype(BF16)
 

time: 23 us -> 23 us (level)
  no operation moved by 1% of the time
where the time goes in v4:
time: 23 us; the launch traced here: 22.8 us
  Pallas kernels  22.2 us (97%)
  between operations  0.64 us (3%)
    pallas_call x1, Pallas kernels, local(): pl.pallas_call(functools.partial(kernel, n, heads, half, width), name='at...  21.3 us
    pallas_call x1, Pallas kernels, local(): pl.pallas_call(place, name='place_grads', out_shape=tuple((pltpu.HBM(g.sh...  0.85 us

profile of v4, /device:TPU:127, one launch (start us, length us, event | category | flops | bytes accessed | tf_op | source)
XLA Modules:
  0.0 22.8 jit_solution(10331667404282103377)
XLA Ops:
  0.6 21.3 %attention_grads.1 = (bf16[256,1024]{1,0:T(8,128)(2,1)S(1)}, bf16[256,128]{1,0:T(8,128)(2,1)S(1)}, bf16[256,128]{1,0:T(8,128)(2,1)S(1)}) custom-call(bf16[256,1024]{1,0:T(8,128)(2,1)} %query_hbm.1, bf16[8,32,128]{2,1,0:T(8,128)(2,1)} %bitcast.2, bf16[8,32,128]{2,1,0:T(8,128)(2,1)} %bitcast.3, bf16[256,1024]{1,0:T(8,128)(2,1)} %grad_hbm.1, ...), custom_call_target="tpu_custom_call" | custom-call | flops 1174405120 | bytes 2097152 | tf_op jit(solution)/shard_map/attention_grads/pallas_call | solution.py:342
  22.0 0.9 %place_grads.1 = (bf16[256,1024]{1,0:T(8,128)(2,1)}, bf16[256,128]{1,0:T(8,128)(2,1)}, bf16[256,128]{1,0:T(8,128)(2,1)}) custom-call(bf16[256,1024]{1,0:T(8,128)(2,1)S(1)} %get-tuple-element.6.query_grad, bf16[256,128]{1,0:T(8,128)(2,1)S(1)} %get-tuple-element.7.key_grad, bf16[256,128]{1,0:T(8,128)(2,1)S(1)} %get-tuple-element.8.value_grad), custom_call_target="tpu_custom_call" | custom-call | tf_op jit(solution)/shard_map/place_grads/pallas_call | solution.py:381

commit v5 on v4

--- a/solution.py
+++ b/solution.py
@@ -77,9 +77,6 @@
     def wait_all(ref, sem):
         pltpu.make_async_copy(ref, ref, sem).wait()
 
-    for which, source in enumerate((key_hbm, value_hbm)):
-        load(source, own.at[:, which], 0)
-
     def near_from_hbm():
         for piece, (first, count) in enumerate(PIECES):
             for which, source in enumerate((key_hbm, value_hbm)):
@@ -97,6 +94,9 @@
         pl.semaphore_wait(barrier, 3)
         tell(ready, lax.rem(me + n - 2, n), via)
         near_from_hbm()
+
+    for which, source in enumerate((key_hbm, value_hbm)):
+        load(source, own.at[:, which], 0)
 
     for which, source in enumerate((query_hbm, grad_hbm)):
         for block in range(2):

time: 23 us -> 23 us (level)
  no operation moved by 1% of the time
where the time goes in v5:
time: 23 us; the launch traced here: 22.8 us
  Pallas kernels  22.2 us (97%)
  between operations  0.64 us (3%)
    pallas_call x1, Pallas kernels, local(): pl.pallas_call(functools.partial(kernel, n, heads, half, width), name='at...  21.3 us
    pallas_call x1, Pallas kernels, local(): pl.pallas_call(place, name='place_grads', out_shape=tuple((pltpu.HBM(g.sh...  0.85 us

profile of v5, /device:TPU:127, one launch (start us, length us, event | category | flops | bytes accessed | tf_op | source)
XLA Modules:
  0.0 22.8 jit_solution(1274518418431556177)
XLA Ops:
  0.6 21.3 %attention_grads.1 = (bf16[256,1024]{1,0:T(8,128)(2,1)S(1)}, bf16[256,128]{1,0:T(8,128)(2,1)S(1)}, bf16[256,128]{1,0:T(8,128)(2,1)S(1)}) custom-call(bf16[256,1024]{1,0:T(8,128)(2,1)} %query_hbm.1, bf16[8,32,128]{2,1,0:T(8,128)(2,1)} %bitcast.2, bf16[8,32,128]{2,1,0:T(8,128)(2,1)} %bitcast.3, bf16[256,1024]{1,0:T(8,128)(2,1)} %grad_hbm.1, ...), custom_call_target="tpu_custom_call" | custom-call | flops 1174405120 | bytes 2097152 | tf_op jit(solution)/shard_map/attention_grads/pallas_call | solution.py:342
  22.0 0.9 %place_grads.1 = (bf16[256,1024]{1,0:T(8,128)(2,1)}, bf16[256,128]{1,0:T(8,128)(2,1)}, bf16[256,128]{1,0:T(8,128)(2,1)}) custom-call(bf16[256,1024]{1,0:T(8,128)(2,1)S(1)} %get-tuple-element.6.query_grad, bf16[256,128]{1,0:T(8,128)(2,1)S(1)} %get-tuple-element.7.key_grad, bf16[256,128]{1,0:T(8,128)(2,1)S(1)} %get-tuple-element.8.value_grad), custom_call_target="tpu_custom_call" | custom-call | tf_op jit(solution)/shard_map/place_grads/pallas_call | solution.py:381
